TPU v7x, 256 devices: a whole 4x4x8 slice. The times are simulated.
256 devices in a mesh: row: 32 (over z, x), col: 8 (over y, core).
Axes of the slice: x: 4, y: 4, z: 8, core: 2. Of those that a mesh axis runs over, the one named last changes fastest.
Arguments:
- blocks: bfloat16 [384, 16, 256, 256], P('row', 'col'), may hold values from -0.09375 to 0.09375
- neighbours: int32 [384, 16], P('row', 'col'), may hold values from 0 to 23, as said below
- start: bfloat16 [98304, 256], P(('row', 'col')), may hold values from -6 to 6
Outputs:
- basis: float32 [98304, 256], P(('row', 'col'))
- diagonal: float32 [256], replicated
Inputs may be any that keep to these rules, and one draw needn't show every extreme that they name: The entries of one row of neighbours are distinct, so the slots of a block row name distinct block columns.
All inputs are finite; a program needn't handle non-finite values.
Results may differ from a plain program's by a relative error of at most 0.007.
Values may be sent and summed in bfloat16 or wider, within the bound.
No kernel may reach another device: no remote copies, remote signals or barrier semaphores. Data moves between devices by JAX's collectives and lax.ppermute only.
A program may use at most 64 MiB of HBM per device.

v0:
```python
import math

import jax
import jax.numpy as jnp
from jax import lax
from jax.sharding import PartitionSpec as P

ITERS = 2


def padded_2(block, sides, width):
    for axis, dim in sides:
        count = lax.axis_size(axis)
        forward = [(i, i + 1) for i in range(count - 1)]
        forward.append((count - 1, 0))
        backward = [(target, source) for source, target in forward]
        low = lax.ppermute(
            lax.slice_in_dim(block, block.shape[dim] - width, None, axis=dim), axis, forward
        )
        high = lax.ppermute(lax.slice_in_dim(block, 0, width, axis=dim), axis, backward)
        block = jnp.concatenate([low, block, high], axis=dim)
    return block


def shifted(value, axis, steps):
    count = lax.axis_size(axis)
    pairs = [(source, (source + steps) % count) for source in range(count)]
    return lax.ppermute(value, axis, pairs)


def per_device(blocks, neighbours, start):
    block_rows = blocks.shape[0]
    side = blocks.shape[2]
    width = start.shape[1]
    half_rows = block_rows // 2
    total_rows = block_rows * side * lax.axis_size("row")
    onehot = (
        neighbours[:, :, None] == jnp.arange(2 * block_rows, dtype=jnp.int32)[None, None, :]
    ).astype(jnp.float32)
    current = start
    for step in range(ITERS):
        group_rows = lax.all_gather(current, "col", axis=0, tiled=True)
        padded = padded_2(group_rows, (("row", 0),), half_rows * side)
        window_x = padded.reshape(2 * block_rows, side, width)
        picked = jnp.take(window_x, neighbours, axis=0)
        partial_value = jnp.einsum(
            "rnab,rnbk->rak", blocks, picked, preferred_element_type=jnp.float32
        )
        image_rows = lax.psum(partial_value, "col").astype(jnp.bfloat16)
        terms = jnp.einsum("rnba,rbk->rnak", blocks, image_rows, preferred_element_type=jnp.float32)
        window = jnp.einsum(
            "rnw,rnak->wak",
            onehot,
            terms,
            precision=lax.Precision.HIGHEST,
            preferred_element_type=jnp.float32,
        )
        lower_part = window[:half_rows]
        own_part = window[half_rows : half_rows + block_rows]
        upper_part = window[half_rows + block_rows :]
        from_prev = shifted(upper_part.astype(jnp.bfloat16), "row", 1).astype(upper_part.dtype)
        from_next = shifted(lower_part.astype(jnp.bfloat16), "row", -1).astype(lower_part.dtype)
        own_part = own_part + jnp.concatenate([from_prev, from_next], axis=0)
        result = lax.psum_scatter(
            own_part.reshape(block_rows * side, width), "col", scatter_dimension=0, tiled=True
        )
        local_gram = jnp.dot(
            result.T, result, precision=lax.Precision.HIGHEST, preferred_element_type=jnp.float32
        )
        gram = lax.psum(local_gram, ("row", "col"))
        lower = jnp.linalg.cholesky(gram)
        basis = lax.linalg.triangular_solve(
            lower, result, left_side=False, lower=True, transpose_a=True
        )
        current = basis.astype(jnp.bfloat16)
    return (basis * math.sqrt(total_rows), jnp.diagonal(lower))


def solution(mesh):
    placed = (P("row", "col", None, None), P("row", "col"), P(("row", "col"), None))
    return jax.shard_map(
        per_device,
        mesh=mesh,
        in_specs=placed,
        out_specs=(P(("row", "col"), None), P()),
        check_vma=False,
    )
```

profile of v0, /device:TPU:2, one launch (start us, length us, event | category | flops | bytes accessed | tf_op | source)
XLA Modules:
  0.0 1129.2 jit_solution(1303876450823438992)
XLA Ops:
  8.0 31.8 %all-gather.3.cloned.1.call-done = bf16[3072,256]{1,0:T(8,128)(2,1)} async-done(((bf16[384,256]{1,0:T(8,128)(2,1)}), bf16[3072,256]{1,0:T(8,128)(2,1)}) %all-gather.3.cloned.1.call-update) | async-done | bytes 1572880 | tf_op jit(solution)/shard_map/all_gather | solution.py:42
  39.7 2.6 fusion.53
  44.7 17.7 %collective-permute-done = bf16[1536,256]{1,0:T(8,128)(2,1)} collective-permute-done((bf16[1536,256]{1,0:T(8,128)(2,1)}, bf16[1536,256]{1,0:T(8,128)(2,1)}, u32[]{:S(2)}, u32[]{:S(2)}) %collective-permute-start) | collective-permute-done | bytes 786464 | tf_op jit(solution)/shard_map/ppermute | solution.py:17
  63.6 3.1 pad_maximum_fusion
  66.7 4.4 gather_fusion.1
  71.1 4.6 copy.29
  75.8 4.6 fusion.6
  80.4 55.1 %all-reduce.9 = bf16[12,256,256]{1,2,0:T(8,128)(2,1)} all-reduce(f32[12,256,256]{1,2,0:T(8,128)} %fusion.6), channel_id=1, replica_groups=mesh['row'=32,'col'=8] {'col'}, use_global_device_ids=true, to_apply=%region_0.0 | all-reduce | flops 786432 | bytes 4718592 | tf_op jit(solution)/shard_map/psum | solution.py:49
  135.4 5.1 convolution_bitcast_fusion.1
  140.5 9.7 copy.30
  150.2 6.5 fusion.54
  158.5 2.6 collective-permute-start.3
  161.1 16.0 %collective-permute-done.2 = bf16[6,256,256]{2,1,0:T(8,128)(2,1)S(1)} collective-permute-done((bf16[6,256,256]{2,1,0:T(8,128)(2,1)S(1)}, bf16[6,256,256]{2,1,0:T(8,128)(2,1)S(1)}, u32[]{:S(2)}, u32[]{:S(2)}) %collective-permute-start.2) | collective-permute-done | bytes 786464 | tf_op jit(solution)/shard_map/ppermute | solution.py:28
  180.6 3.5 copy.35
  184.2 40.1 %reduce-scatter.3.cloned.1.call-done = f32[384,256]{1,0:T(8,128)} async-done(((f32[3072,256]{1,0:T(8,128)}), f32[384,256]{1,0:T(8,128)}) %reduce-scatter.3.cloned.1.call-update) | async-done | bytes 393232 | tf_op jit(solution)/shard_map/reduce_scatter | solution.py:64
  224.3 2.7 fusion.56
  227.6 252.0 %all-reduce.6.cloned.1.call-done = f32[256,256]{0,1:T(8,128)} async-done(((f32[256,256]{0,1:T(8,128)}), f32[256,256]{0,1:T(8,128)}) %all-reduce.6.cloned.1.call-update) | async-done | bytes 262160 | tf_op jit(solution)/shard_map/psum | solution.py:70
  483.7 13.2 %cholesky.130 = f32[128,128]{1,0:T(8,128)} custom-call(f32[128,128]{1,0:T(8,128)} %cholesky.194), custom_call_target="Cholesky" | custom-call | tf_op jit(solution)/shard_map/jit(cholesky)/cholesky | solution.py:71
  498.4 11.3 custom-call.15
  514.7 13.2 %cholesky.147 = f32[128,128]{1,0:T(8,128)} custom-call(f32[128,128]{1,0:T(8,128)} %convolution_subtract_fusion.3), custom_call_target="Cholesky" | custom-call | tf_op jit(solution)/shard_map/jit(cholesky)/cholesky | solution.py:71
  534.3 15.8 %while.4 = (s32[]{:T(128)}, f32[256,256]{1,0:T(8,128)}, s32[2,2]{1,0:T(2,128)S(1)}, f32[2,128,128]{2,1,0:T(8,128)}, s32[]{:T(128)}) while((s32[]{:T(128)}, f32[256,256]{1,0:T(8,128)}, s32[2,2]{1,0:T(2,128)S(1)}, f32[2,128,128]{2,1,0:T(8,128)}, s32[]{:T(128)}) %tuple.58), condition=%wide.while_cond, body=%wide.while_body.sunk | while | flops 2 | bytes 132705 | solution.py:72
  543.5 3.0 bitcast_dynamic-update-slice_fusion.4
  547.1 2.9 bitcast_dynamic-update-slice_fusion.4
  550.1 21.1 %custom-call.16 = f32[2,128,128]{1,2,0:T(8,128)} custom-call(f32[2,128,128]{2,1,0:T(8,128)} %get-tuple-element.19), custom_call_target="InvertDiagBlocksLowerTriangular" | custom-call | tf_op jit(solution)/shard_map/triangular_solve/custom-call.0 | solution.py:72
  575.8 26.0 %all-gather.5.cloned.1.call-done = bf16[3072,256]{0,1:T(8,128)(2,1)} async-done(((bf16[384,256]{0,1:T(8,128)(2,1)}), bf16[3072,256]{0,1:T(8,128)(2,1)}) %all-gather.5.cloned.1.call-update) | async-done | bytes 1572880 | tf_op jit(solution)/shard_map/all_gather | solution.py:42
  605.5 17.7 %collective-permute-done.4 = bf16[1536,256]{0,1:T(8,128)(2,1)S(1)} collective-permute-done((bf16[1536,256]{0,1:T(8,128)(2,1)S(1)}, bf16[1536,256]{0,1:T(8,128)(2,1)S(1)}, u32[]{:S(2)}, u32[]{:S(2)}) %collective-permute-start.4) | collective-permute-done | bytes 786464 | tf_op jit(solution)/shard_map/ppermute | solution.py:17
  626.2 4.6 copy.58
  630.8 4.4 gather_fusion.2
  635.2 4.6 copy.40
  639.9 4.6 fusion.9
  644.5 55.1 %all-reduce.10 = bf16[12,256,256]{1,2,0:T(8,128)(2,1)} all-reduce(f32[12,256,256]{1,2,0:T(8,128)} %fusion.9), channel_id=1, replica_groups=mesh['row'=32,'col'=8] {'col'}, use_global_device_ids=true, to_apply=%region_7.11 | all-reduce | flops 786432 | bytes 4718592 | tf_op jit(solution)/shard_map/psum | solution.py:49
  699.5 5.1 convolution_bitcast_fusion
  704.6 9.7 copy.41
  714.3 6.5 fusion.55
  722.8 2.3 collective-permute-start.7
  725.1 16.3 %collective-permute-done.6 = bf16[6,256,256]{2,1,0:T(8,128)(2,1)S(1)} collective-permute-done((bf16[6,256,256]{2,1,0:T(8,128)(2,1)S(1)}, bf16[6,256,256]{2,1,0:T(8,128)(2,1)S(1)}, u32[]{:S(2)}, u32[]{:S(2)}) %collective-permute-start.6) | collective-permute-done | bytes 786464 | tf_op jit(solution)/shard_map/ppermute | solution.py:28
  744.7 3.5 copy.46
  748.2 40.1 %reduce-scatter.5.cloned.1.call-done = f32[384,256]{1,0:T(8,128)} async-done(((f32[3072,256]{1,0:T(8,128)}), f32[384,256]{1,0:T(8,128)}) %reduce-scatter.5.cloned.1.call-update) | async-done | bytes 393232 | tf_op jit(solution)/shard_map/reduce_scatter | solution.py:64
  788.3 2.7 fusion.57
  791.0 252.4 %all-reduce.8.cloned.1.call-done = f32[256,256]{0,1:T(8,128)} async-done(((f32[256,256]{0,1:T(8,128)}), f32[256,256]{0,1:T(8,128)}) %all-reduce.8.cloned.1.call-update) | async-done | bytes 262160 | tf_op jit(solution)/shard_map/psum | solution.py:70
  1046.1 11.7 %cholesky.164 = f32[128,128]{1,0:T(8,128)S(1)} custom-call(f32[128,128]{1,0:T(8,128)S(1)} %cholesky.197), custom_call_target="Cholesky" | custom-call | tf_op jit(solution)/shard_map/jit(cholesky)/cholesky | solution.py:71
  1057.9 9.8 custom-call.17
  1069.9 11.7 %cholesky.181 = f32[128,128]{1,0:T(8,128)S(1)} custom-call(f32[128,128]{1,0:T(8,128)S(1)} %convolution_subtract_fusion.2), custom_call_target="Cholesky" | custom-call | tf_op jit(solution)/shard_map/jit(cholesky)/cholesky | solution.py:71
  1086.0 6.0 while.5
  1086.9 2.3 bitcast_dynamic-update-slice_fusion.5
  1089.8 2.2 bitcast_dynamic-update-slice_fusion.5
  1092.6 20.5 %custom-call.18 = f32[2,128,128]{1,2,0:T(8,128)S(1)} custom-call(f32[2,128,128]{2,1,0:T(8,128)} %copy-done.6), custom_call_target="InvertDiagBlocksLowerTriangular" | custom-call | tf_op jit(solution)/shard_map/triangular_solve/custom-call.0 | solution.py:72
  1119.0 2.9 gather_fusion
  (101 shorter events, 59.9 us)
Async XLA Ops:
  7.2 68.6 %copy-start = (bf16[12,2,256,256]{3,2,1,0:T(8,128)(2,1)S(1)}, bf16[12,2,256,256]{3,2,1,0:T(8,128)(2,1)}, u32[]{:S(2)}) copy-start(bf16[12,2,256,256]{3,2,1,0:T(8,128)(2,1)} %param.8) | copy-start | bytes 9437188
  7.2 37.2 %copy-start.7 = (s32[12,2]{0,1:T(2,128)S(1)}, s32[12,2]{0,1:T(2,128)}, u32[]{:S(2)}) copy-start(s32[12,2]{0,1:T(2,128)} %param.9) | copy-start | bytes 292
  7.2 32.5 %all-gather.3.cloned.1.call-start = ((), (), s32[]{:S(2)}) async-start(), calls=%async_computation.2 | async-start | bytes 1769472 | tf_op jit(solution)/shard_map/all_gather | solution.py:42
  7.9 216.3 %reduce-scatter.3.cloned.1.call-start = ((), (), s32[]{:S(2)}) async-start(), calls=%async_computation.3 | async-start | bytes 3538944 | tf_op jit(solution)/shard_map/reduce_scatter | solution.py:64
  42.4 20.0 %collective-permute-start = (bf16[1536,256]{1,0:T(8,128)(2,1)}, bf16[1536,256]{1,0:T(8,128)(2,1)}, u32[]{:S(2)}, u32[]{:S(2)}) collective-permute-start(bf16[1536,256]{1,0:T(8,128)(2,1)} %get-tuple-element.55), channel_id=1, source_target_pairs={{0,8},{8,16},{16,24},{24,32},{32,40},{40,48},{48,56},{56,64},{64,7... | collective-permute-start | bytes 2359304 | tf_op jit(solution)/shard_map/ppermute | solution.py:17
  43.8 19.7 %collective-permute-start.1 = (bf16[1536,256]{1,0:T(8,128)(2,1)}, bf16[1536,256]{1,0:T(8,128)(2,1)}, u32[]{:S(2)}, u32[]{:S(2)}) collective-permute-start(bf16[1536,256]{1,0:T(8,128)(2,1)} %get-tuple-element.56), channel_id=1, source_target_pairs={{8,0},{16,8},{24,16},{32,24},{40,32},{48,40},{56,48},{64,56},{72,6... | collective-permute-start | bytes 2359304 | tf_op jit(solution)/shard_map/ppermute | solution.py:20
  157.1 20.0 %collective-permute-start.2 = (bf16[6,256,256]{2,1,0:T(8,128)(2,1)S(1)}, bf16[6,256,256]{2,1,0:T(8,128)(2,1)S(1)}, u32[]{:S(2)}, u32[]{:S(2)}) collective-permute-start(bf16[6,256,256]{2,1,0:T(8,128)(2,1)S(1)} %copy.31), channel_id=1, source_target_pairs={{0,8},{8,16},{16,24},{24,32},{32,40},{40,48},{48,56},{56,64},{64,7... | collective-permute-start | bytes 2359304 | tf_op jit(solution)/shard_map/ppermute | solution.py:28
  158.5 20.5 %collective-permute-start.3 = (bf16[6,256,256]{2,1,0:T(8,128)(2,1)S(1)}, bf16[6,256,256]{2,1,0:T(8,128)(2,1)S(1)}, u32[]{:S(2)}, u32[]{:S(2)}) collective-permute-start(bf16[6,256,256]{2,1,0:T(8,128)(2,1)S(1)} %copy.32), channel_id=1, source_target_pairs={{0,248},{8,0},{16,8},{24,16},{32,24},{40,32},{48,40},{56,48},{64,5... | collective-permute-start | bytes 2359304 | tf_op jit(solution)/shard_map/ppermute | solution.py:28
  184.1 295.4 %all-reduce.6.cloned.1.call-start = ((), (), s32[]{:S(2)}) async-start(), calls=%async_computation.4 | async-start | bytes 524288 | tf_op jit(solution)/shard_map/psum | solution.py:70
  224.3 346.9 %copy-start.2 = (f32[384,256]{1,0:T(8,128)S(1)}, f32[384,256]{1,0:T(8,128)}, u32[]{:S(2)}) copy-start(f32[384,256]{1,0:T(8,128)} %reduce-scatter.3.cloned.1.call-done) | copy-start | bytes 1179652
  227.0 374.8 %all-gather.5.cloned.1.call-start = ((), (), s32[]{:S(2)}) async-start(), calls=%async_computation.5 | async-start | bytes 1769472 | tf_op jit(solution)/shard_map/all_gather | solution.py:42
  482.4 0.7 copy-start.4
  575.7 212.5 %reduce-scatter.5.cloned.1.call-start = ((), (), s32[]{:S(2)}) async-start(), calls=%async_computation.6 | async-start | bytes 3538944 | tf_op jit(solution)/shard_map/reduce_scatter | solution.py:64
  601.8 22.6 %copy-start.1 = (bf16[3072,256]{0,1:T(8,128)(2,1)S(1)}, bf16[3072,256]{0,1:T(8,128)(2,1)}, u32[]{:S(2)}) copy-start(bf16[3072,256]{0,1:T(8,128)(2,1)} %all-gather.5.cloned.1.call-done) | copy-start | bytes 4718596
  603.4 19.8 %collective-permute-start.4 = (bf16[1536,256]{0,1:T(8,128)(2,1)S(1)}, bf16[1536,256]{0,1:T(8,128)(2,1)S(1)}, u32[]{:S(2)}, u32[]{:S(2)}) collective-permute-start(bf16[1536,256]{0,1:T(8,128)(2,1)S(1)} %get-tuple-element.53), channel_id=1, source_target_pairs={{0,8},{8,16},{16,24},{24,32},{32,40},{40,48},{48,56},{56,64},{64,7... | collective-permute-start | bytes 2359304 | tf_op jit(solution)/shard_map/ppermute | solution.py:17
  604.9 19.4 %collective-permute-start.5 = (bf16[1536,256]{0,1:T(8,128)(2,1)S(1)}, bf16[1536,256]{0,1:T(8,128)(2,1)S(1)}, u32[]{:S(2)}, u32[]{:S(2)}) collective-permute-start(bf16[1536,256]{0,1:T(8,128)(2,1)S(1)} %get-tuple-element.54), channel_id=1, source_target_pairs={{8,0},{16,8},{24,16},{32,24},{40,32},{48,40},{56,48},{64,56},{72,6... | collective-permute-start | bytes 2359304 | tf_op jit(solution)/shard_map/ppermute | solution.py:20
  721.2 20.2 %collective-permute-start.6 = (bf16[6,256,256]{2,1,0:T(8,128)(2,1)S(1)}, bf16[6,256,256]{2,1,0:T(8,128)(2,1)S(1)}, u32[]{:S(2)}, u32[]{:S(2)}) collective-permute-start(bf16[6,256,256]{2,1,0:T(8,128)(2,1)S(1)} %copy.42), channel_id=1, source_target_pairs={{0,8},{8,16},{16,24},{24,32},{32,40},{40,48},{48,56},{56,64},{64,7... | collective-permute-start | bytes 2359304 | tf_op jit(solution)/shard_map/ppermute | solution.py:28
  722.8 20.3 %collective-permute-start.7 = (bf16[6,256,256]{2,1,0:T(8,128)(2,1)S(1)}, bf16[6,256,256]{2,1,0:T(8,128)(2,1)S(1)}, u32[]{:S(2)}, u32[]{:S(2)}) collective-permute-start(bf16[6,256,256]{2,1,0:T(8,128)(2,1)S(1)} %copy.43), channel_id=1, source_target_pairs={{0,248},{8,0},{16,8},{24,16},{32,24},{40,32},{48,40},{56,48},{64,5... | collective-permute-start | bytes 2359304 | tf_op jit(solution)/shard_map/ppermute | solution.py:28
  748.2 295.2 %all-reduce.8.cloned.1.call-start = ((), (), s32[]{:S(2)}) async-start(), calls=%async_computation.7 | async-start | bytes 524288 | tf_op jit(solution)/shard_map/psum | solution.py:70
  1045.4 0.7 copy-start.5
  1081.6 2.6 copy-start.3
  1092.0 0.6 copy-start.6
Sparse Core Ops, SparseCore 0:
  9.9 29.8 all-gather.2
  184.2 39.9 reduce-scatter.2
  230.3 249.1 all-reduce.5
  575.8 25.8 all-gather.4
  748.3 39.9 reduce-scatter.4
  794.2 249.1 all-reduce.7
where the time goes:
time: 1140 us; the launch traced here: 1130 us
  waiting for transfers between devices  716 us (63%)
  other arithmetic  132 us (12%)
  blocking collectives  110 us (10%)
  local copies, waits for them, and re-layouts  82.7 us (7%)
  matrix products  50.2 us (4%)
  between operations  17.4 us (2%)
  starting transfers between devices  12 us (1%)
    psum x2, waiting for transfers between devices, per_device(): gram = lax.psum(local_gram, ('row', 'col'))  504 us
    psum x2, blocking collectives, per_device(): image_rows = lax.psum(partial_value, 'col').astype(jnp.bfloat16)  110 us
    reduce_scatter x2, waiting for transfers between devices, per_device(): lax.psum_scatter(own_part.reshape(block_rows * side, width), 'col', scatt...  80.2 us
    another operation x13, other arithmetic, per_device(): lower = jnp.linalg.cholesky(gram)  76 us
    all_gather x2, waiting for transfers between devices, per_device(): group_rows = lax.all_gather(current, 'col', axis=0, tiled=True)  57.8 us
    another operation x5, other arithmetic, per_device(): lax.linalg.triangular_solve(lower, result, left_side=False, lower=True, t...  45.5 us
    ppermute x2, waiting for transfers between devices, padded_2(): lax.ppermute(lax.slice_in_dim(block, block.shape[dim] - width, None, axis...  35.4 us
    ppermute x4, waiting for transfers between devices, shifted(): return lax.ppermute(value, axis, pairs)  35 us
  transfers between devices with their start and end apart: 14, of which 14 were waited for; matrix products, arithmetic and copies ran while one was open for 0% of the time, Pallas kernels for 0%

commit v1 on v0

v1 whole, which is shorter than its diff:
```python
import functools
import math

import jax
import jax.numpy as jnp
from jax import lax
from jax.experimental import pallas as pl
from jax.experimental.pallas import tpu as pltpu
from jax.sharding import PartitionSpec as P

ITERS = 2
PANEL = 64
GROUP = 4
HIGH = lax.Precision.HIGHEST


def band_kernel(cols, halves, slots, nb_ref, blk_ref, x_ref, out_ref, xwin, zacc, zbf, yref, sem):
    piece = x_ref.shape[0] // (2 * cols)
    side = 2 * blk_ref.shape[3]
    half = side // 2
    low = cols // 2 * piece
    places = []
    for c in range(cols):
        places.append((c * 2 * piece, low + c * piece))
        at = low + cols * piece + c * piece if c < cols // 2 else (c - cols // 2) * piece
        places.append((c * 2 * piece + piece, at))
    ins = [
        pltpu.make_async_copy(x_ref.at[pl.ds(a, piece)], xwin.at[pl.ds(b, piece)], sem.at[i])
        for i, (a, b) in enumerate(places)
    ]
    for copy in ins:
        copy.start()
    zacc[...] = jnp.zeros_like(zacc)
    for copy in ins:
        copy.wait()
    per = halves * slots
    for h in range(halves):

        def forward(s, acc):
            for n in range(slots):
                w = nb_ref[s * per + h * slots + n]
                x = xwin[pl.ds(pl.multiple_of(w * side, side), side), :]
                acc = acc + jnp.dot(blk_ref[s, h, n], x, preferred_element_type=jnp.float32)
            return acc

        acc = lax.fori_loop(0, cols, forward, jnp.zeros((half, xwin.shape[1]), jnp.float32))
        yref[h] = acc.astype(jnp.bfloat16)

    def back(s, carry):
        for h in range(halves):
            for n in range(slots):
                w = nb_ref[s * per + h * slots + n]
                term = lax.dot_general(
                    blk_ref[s, h, n],
                    yref[h],
                    (((0,), (0,)), ((), ())),
                    preferred_element_type=jnp.float32,
                )
                zacc[pl.ds(pl.multiple_of(w * side, side), side), :] += term
        return carry

    lax.fori_loop(0, cols, back, 0)
    outs = [
        pltpu.make_async_copy(zbf.at[pl.ds(b, piece)], out_ref.at[pl.ds(a, piece)], sem.at[i])
        for i, (a, b) in enumerate(places)
    ]
    for copy, (a, b) in zip(outs, places):
        zbf[pl.ds(b, piece), :] = zacc[pl.ds(b, piece), :].astype(jnp.bfloat16)
        copy.start()
    for copy in outs:
        copy.wait()


def band(nb, blk, x):
    cols, halves, slots, half, side = blk.shape
    width = x.shape[1]
    window = x.shape[0]
    return pl.pallas_call(
        functools.partial(band_kernel, cols, halves, slots),
        out_shape=jax.ShapeDtypeStruct(x.shape, jnp.bfloat16),
        in_specs=[
            pl.BlockSpec(memory_space=pltpu.SMEM),
            pl.BlockSpec(memory_space=pltpu.VMEM),
            pl.BlockSpec(memory_space=pl.ANY),
        ],
        out_specs=pl.BlockSpec(memory_space=pl.ANY),
        scratch_shapes=[
            pltpu.VMEM((window, width), jnp.bfloat16),
            pltpu.VMEM((window, width), jnp.float32),
            pltpu.VMEM((window, width), jnp.bfloat16),
            pltpu.VMEM((halves, half, width), jnp.bfloat16),
            pltpu.SemaphoreType.DMA((2 * cols,)),
        ],
        compiler_params=pltpu.CompilerParams(vmem_limit_bytes=40 * 2**20),
        name="band",
    )(nb, blk, x)


def gram_kernel(rs_ref, got_ref, z_ref, g_ref):
    piece = got_ref.shape[0]
    z = rs_ref[:piece, :].astype(jnp.float32) + got_ref[...].astype(jnp.float32)
    z_ref[...] = z
    g_ref[...] = lax.dot_general(
        z, z, (((0,), (0,)), ((), ())), precision=HIGH, preferred_element_type=jnp.float32
    )


def gram(rs, got):
    width = rs.shape[1]
    return pl.pallas_call(
        gram_kernel,
        out_shape=(
            jax.ShapeDtypeStruct(got.shape, jnp.float32),
            jax.ShapeDtypeStruct((width, width), jnp.float32),
        ),
        name="gram",
    )(rs, got)


def panel(tiles, start, count):
    lanes = 128
    at, offset = start // lanes, start % lanes
    rows = lax.broadcasted_iota(jnp.int32, (count, lanes), 0)
    pivots = jnp.ones((count, lanes), jnp.float32)
    for k in range(0, count, GROUP):
        columns = [
            jnp.broadcast_to(
                tiles[at][:, offset + k + j : offset + k + j + 1], (count, lanes)
            )
            for j in range(GROUP)
        ]
        heads = [[t[k + j : k + j + 1, :] for t in tiles] for j in range(GROUP)]
        terms = []
        for j in range(GROUP):
            pivot = columns[j][k + j : k + j + 1, :]
            inverse = 1.0 / pivot
            scaled = [h * inverse for h in heads[j]]
            below = jnp.where(rows > k + j, columns[j], 0.0)
            terms.append((below, scaled))
            pivots = jnp.where(rows == k + j, pivot, pivots)
            for i in range(j + 1, GROUP):
                factor = columns[j][k + i : k + i + 1, :]
                columns[i] = columns[i] - columns[j] * (factor * inverse)
                heads[i] = [h - factor * s for h, s in zip(heads[i], scaled)]
        for t in range(len(tiles)):
            total = tiles[t]
            for below, scaled in terms:
                total = total - below * scaled[t]
            tiles[t] = total
    scale = 1.0 / jnp.sqrt(pivots)
    return [t * scale for t in tiles]


def orthonormal_kernel(factor, g_ref, z_ref, q_ref, d_ref, m):
    width = g_ref.shape[0]
    lanes = 128
    m[:, :width] = g_ref[...]
    r = lax.broadcasted_iota(jnp.int32, (width, width), 0)
    c = lax.broadcasted_iota(jnp.int32, (width, width), 1)
    eye = (r == c).astype(jnp.float32)
    m[:, width:] = eye
    for start in range(0, width, PANEL):
        end = start + PANEL
        first = start // lanes
        used = list(range(first, width // lanes)) + list(
            range(width // lanes, width // lanes + (end + lanes - 1) // lanes)
        )
        tiles = [m[start:end, t * lanes : (t + 1) * lanes] for t in used]
        tiles = panel(tiles, start - first * lanes, PANEL)
        for t, value in zip(used, tiles):
            m[start:end, t * lanes : (t + 1) * lanes] = value
        if end < width:
            upper = jnp.concatenate(tiles, axis=1)
            left = upper[:, : width - first * lanes]
            update = lax.dot_general(
                left, upper, (((0,), (0,)), ((), ())), precision=HIGH,
                preferred_element_type=jnp.float32,
            )
            skip = end - first * lanes
            for i, t in enumerate(used):
                m[end:, t * lanes : (t + 1) * lanes] -= update[skip:, i * lanes : (i + 1) * lanes]
    d_ref[...] = jnp.sum(m[:, :width] * eye, axis=0, keepdims=True)
    q = lax.dot_general(
        z_ref[...], m[:, width:], (((1,), (1,)), ((), ())), precision=HIGH,
        preferred_element_type=jnp.float32,
    )
    q_ref[...] = (q * factor).astype(q_ref.dtype)


def orthonormal(g, z, dtype, factor):
    width = g.shape[0]
    return pl.pallas_call(
        functools.partial(orthonormal_kernel, factor),
        out_shape=(
            jax.ShapeDtypeStruct(z.shape, dtype),
            jax.ShapeDtypeStruct((1, width), jnp.float32),
        ),
        scratch_shapes=[pltpu.VMEM((width, 2 * width), jnp.float32)],
        name="orthonormal",
    )(g, z)


def exchange(value, mask, axis, count):
    return lax.ppermute(value, axis, [(i, i ^ mask) for i in range(count)])


def summed(value):
    cols = lax.axis_size("col")
    count = lax.axis_size("row")
    parts = lax.all_to_all(value, "col", 0, 0, tiled=True)
    part = jnp.sum(parts.reshape((cols, -1) + value.shape[1:]), axis=0)
    mask = 1
    while mask < count:
        part = part + exchange(part, mask, "row", count)
        mask *= 2
    return lax.all_to_all(jnp.tile(part, (cols, 1)), "col", 0, 0, tiled=True)


def per_device(blocks, neighbours, start):
    rows, slots, side, _ = blocks.shape
    cols = lax.axis_size("col")
    groups = lax.axis_size("row")
    piece, width = start.shape
    total_rows = piece * cols * groups
    half = side // 2
    halves = 2 * rows // cols

    def hop(g, c):
        return ((g - 1) % groups if c < cols // 2 else (g + 1) % groups) * cols + c

    out_hop = [(g * cols + c, hop(g, c)) for g in range(groups) for c in range(cols)]
    back_hop = [(b, a) for a, b in out_hop]

    sent = blocks.reshape(rows, slots, 2, half, side).transpose(0, 2, 1, 3, 4)
    sent = sent.reshape(cols, halves * slots * half, side)
    numbers = jnp.broadcast_to(neighbours[:, None, :], (rows, 2, slots))
    numbers = numbers.reshape(cols, 1, halves * slots).astype(jnp.bfloat16)
    numbers = jnp.pad(numbers, ((0, 0), (0, 15), (0, side - halves * slots)))
    sent = jnp.concatenate([sent, numbers], axis=1)
    got = lax.all_to_all(sent, "col", 0, 0, tiled=True)
    blk = got[:, :-16].reshape(cols, halves, slots, half, side)
    nb = got[:, -16, : halves * slots].astype(jnp.int32).reshape(-1)

    current = start
    for step in range(ITERS):
        halo = lax.ppermute(current, ("row", "col"), out_hop)
        window = lax.all_gather(
            jnp.concatenate([current, halo], axis=0), "col", axis=0, tiled=True
        )
        terms = band(nb, blk, window)
        mine = lax.psum_scatter(terms, "col", scatter_dimension=0, tiled=True)
        returned = lax.ppermute(mine[piece:], ("row", "col"), back_hop)
        z, local = gram(mine, returned)
        g = summed(local)
        last = step == ITERS - 1
        current, diagonal = orthonormal(
            g, z, jnp.float32 if last else jnp.bfloat16, math.sqrt(total_rows) if last else 1.0
        )
    return current, diagonal.reshape(width)


def solution(mesh):
    placed = (P("row", "col", None, None), P("row", "col"), P(("row", "col"), None))
    return jax.shard_map(
        per_device,
        mesh=mesh,
        in_specs=placed,
        out_specs=(P(("row", "col"), None), P()),
        check_vma=False,
    )
```

time: 1140 us -> 393 us (0.34)
  waiting for transfers between devices: 716 us -> 161 us
  other arithmetic: 132 us -> 3.73 us
  local copies, waits for them, and re-layouts: 82.7 us -> 16.4 us
  Pallas kernels: 0 us -> 64.3 us
  matrix products: 50.2 us -> 0 us
  starting transfers between devices: 12 us -> 31.3 us
    psum x2 -> x0, waiting for transfers between devices: 504 us -> none  [per_device(): gram = lax.psum(local_gram, ('row', 'col'))]
    another operation x18 -> x0, other arithmetic: 121 us -> none  [the longest x13 76 us: per_device(): lower = jnp.linalg.cholesky(gram)]
    psum x2 -> x0, blocking collectives: 110 us -> none  [per_device(): image_rows = lax.psum(partial_value, 'col').astype(jnp.bfloat16)]
    all_to_all x0 -> x5, blocking collectives: none -> 99.2 us  [the longest x1 56.3 us: per_device(): got = lax.all_to_all(sent, 'col', 0, 0, tiled=True)]
    pallas_call x0 -> x6, Pallas kernels: none -> 64.3 us  [the longest x2 35.1 us: band(): pl.pallas_call(functools.partial(band_kernel, cols, halves, slots), out_s...]
    dot_general x8 -> x0, matrix products: 37.7 us -> none  [the longest x2 12.9 us: per_device(): jnp.einsum('rnw,rnak->wak', onehot, terms, precision=lax.Precision.HIGHES...]
    all_gather x2, waiting for transfers between devices: 57.8 us -> 32.2 us  [per_device(): lax.all_gather(jnp.concatenate([current, halo], axis=0), 'col', axis=0, t...]
    ppermute x8 -> x14, waiting for transfers between devices: 72.8 us -> 50.3 us  [the longest x10 32.8 us: exchange(): return lax.ppermute(value, axis, [(i, i ^ mask) for i in range(count)])]
  transfers between devices with their start and end apart: 14 -> 18, of which waited for: 14 -> 17; matrix products, arithmetic and copies ran while one was open for 0% -> 1% of each run, Pallas kernels for 0% -> 0%
where the time goes in v1:
time: 393 us; the launch traced here: 390 us
  waiting for transfers between devices  161 us (41%)
  blocking collectives  99.2 us (25%)
  Pallas kernels  64.3 us (16%)
  starting transfers between devices  31.3 us (8%)
  local copies, waits for them, and re-layouts  16.4 us (4%)
  between operations  13.9 us (4%)
    reduce_scatter x2, waiting for transfers between devices, per_device(): mine = lax.psum_scatter(terms, 'col', scatter_dimension=0, tiled=True)  78.6 us
    all_to_all x1, blocking collectives, per_device(): got = lax.all_to_all(sent, 'col', 0, 0, tiled=True)  56.3 us
    pallas_call x2, Pallas kernels, band(): pl.pallas_call(functools.partial(band_kernel, cols, halves, slots), out_s...  35.1 us
    ppermute x10, waiting for transfers between devices, exchange(): return lax.ppermute(value, axis, [(i, i ^ mask) for i in range(count)])  32.8 us
    all_gather x2, waiting for transfers between devices, per_device(): lax.all_gather(jnp.concatenate([current, halo], axis=0), 'col', axis=0, t...  32.2 us
    pallas_call x2, Pallas kernels, orthonormal(): pl.pallas_call(functools.partial(orthonormal_kernel, factor), out_shape=(...  24.4 us
    ppermute x10, starting transfers between devices, exchange(): return lax.ppermute(value, axis, [(i, i ^ mask) for i in range(count)])  23.7 us
    all_to_all x2, blocking collectives, summed(): parts = lax.all_to_all(value, 'col', 0, 0, tiled=True)  21.7 us
  transfers between devices with their start and end apart: 18, of which 17 were waited for; matrix products, arithmetic and copies ran while one was open for 1% of the time, Pallas kernels for 0%

profile of v1, /device:TPU:2, one launch (start us, length us, event | category | flops | bytes accessed | tf_op | source)
XLA Modules:
  0.0 390.0 jit_solution(3036877890282575213)
XLA Ops:
  7.2 2.3 collective-permute-start
  9.6 4.6 %collective-permute-done = bf16[384,256]{1,0:T(8,128)(2,1)S(1)} collective-permute-done((bf16[384,256]{1,0:T(8,128)(2,1)}, bf16[384,256]{1,0:T(8,128)(2,1)S(1)}, u32[]{:S(2)}, u32[]{:S(2)}) %collective-permute-start) | collective-permute-done | bytes 196640 | tf_op jit(solution)/shard_map/ppermute | solution.py:246
  14.1 1.7 pad_maximum_fusion
  15.9 2.1 copy.9
  18.5 56.3 %all_to_all.39 = bf16[8,784,256]{2,1,0:T(8,128)(2,1)S(1)} all-to-all(bf16[8,784,256]{2,1,0:T(8,128)(2,1)S(1)} %fusion.1), channel_id=1, replica_groups=mesh['row'=32,'col'=8] {'col'}, dimensions={0} | all-to-all | bytes 6422528 | tf_op jit(solution)/shard_map/all_to_all | solution.py:240
  74.8 1.6 copy-done.4
  76.5 2.1 slice.17
  78.7 1.9 copy-done.2
  80.6 17.6 %band.2 = bf16[6144,256]{1,0:T(8,128)(2,1)S(1)} custom-call(s32[48]{0:T(128)S(1)} %reshape.61.nb_ref, bf16[8,3,2,128,256]{4,3,2,1,0:T(8,128)(2,1)S(1)} %bitcast.10, bf16[6144,256]{1,0:T(8,128)(2,1)S(1)} %copy-done.2), custom_call_target="tpu_custom_call" | custom-call | tf_op jit(solution)/shard_map/band/pallas_call | solution.py:78
  98.1 1.6 copy-done
  99.8 40.1 %reduce-scatter.3.cloned.1.call-done.rs_ref = bf16[768,256]{1,0:T(8,128)(2,1)} async-done(((bf16[6144,256]{1,0:T(8,128)(2,1)}), bf16[768,256]{1,0:T(8,128)(2,1)}) %reduce-scatter.3.cloned.1.call-update) | async-done | bytes 393232 | tf_op jit(solution)/shard_map/reduce_scatter | solution.py:251
  140.9 1.5 collective-permute-start.1
  142.4 4.2 %collective-permute-done.1.got_ref = bf16[384,256]{1,0:T(8,128)(2,1)S(1)} collective-permute-done((bf16[384,256]{1,0:T(8,128)(2,1)S(1)}, bf16[384,256]{1,0:T(8,128)(2,1)S(1)}, u32[]{:S(2)}, u32[]{:S(2)}) %collective-permute-start.1) | collective-permute-done | bytes 196640 | tf_op jit(solution)/shard_map/ppermute | solution.py:252
  147.3 2.4 gram.2
  149.7 10.8 %all_to_all.40 = f32[8,32,256]{2,1,0:T(8,128)S(1)} all-to-all(f32[8,32,256]{2,1,0:T(8,128)} %bitcast.16), channel_id=1, replica_groups=mesh['row'=32,'col'=8] {'col'}, dimensions={0} | all-to-all | bytes 524288 | tf_op jit(solution)/shard_map/all_to_all | solution.py:210
  160.6 4.1 %collective-permute-start.2 = (f32[32,256]{1,0:T(8,128)S(1)}, f32[32,256]{1,0:T(8,128)S(1)}, u32[]{:S(2)}, u32[]{:S(2)}) collective-permute-start(f32[32,256]{1,0:T(8,128)S(1)} %reduce_sum.18), channel_id=1, source_target_pairs={{0,8},{8,0},{16,24},{24,16},{32,40},{40,32},{48,56},{56,48},{64,72... | collective-permute-start | bytes 98312 | tf_op jit(solution)/shard_map/ppermute | solution.py:204
  164.7 1.9 collective-permute-done.2
  166.6 1.0 collective-permute-start.3
  167.6 4.4 %collective-permute-done.3 = f32[32,256]{1,0:T(8,128)S(1)} collective-permute-done((f32[32,256]{1,0:T(8,128)S(1)}, f32[32,256]{1,0:T(8,128)S(1)}, u32[]{:S(2)}, u32[]{:S(2)}) %collective-permute-start.3) | collective-permute-done | bytes 32800 | tf_op jit(solution)/shard_map/ppermute | solution.py:204
  172.2 4.1 %collective-permute-done.4 = f32[32,256]{1,0:T(8,128)S(1)} collective-permute-done((f32[32,256]{1,0:T(8,128)S(1)}, f32[32,256]{1,0:T(8,128)S(1)}, u32[]{:S(2)}, u32[]{:S(2)}) %collective-permute-start.4) | collective-permute-done | bytes 32800 | tf_op jit(solution)/shard_map/ppermute | solution.py:204
  177.1 3.9 %collective-permute-done.5 = f32[32,256]{1,0:T(8,128)S(1)} collective-permute-done((f32[32,256]{1,0:T(8,128)S(1)}, f32[32,256]{1,0:T(8,128)S(1)}, u32[]{:S(2)}, u32[]{:S(2)}) %collective-permute-start.5) | collective-permute-done | bytes 32800 | tf_op jit(solution)/shard_map/ppermute | solution.py:204
  181.1 5.6 %collective-permute-start.6 = (f32[32,256]{1,0:T(8,128)S(1)}, f32[32,256]{1,0:T(8,128)S(1)}, u32[]{:S(2)}, u32[]{:S(2)}) collective-permute-start(f32[32,256]{1,0:T(8,128)S(1)} %add.39), channel_id=1, source_target_pairs={{0,128},{8,136},{16,144},{24,152},{32,160},{40,168},{48,176},{56,1... | collective-permute-start | bytes 98312 | tf_op jit(solution)/shard_map/ppermute | solution.py:204
  186.7 2.2 collective-permute-done.6
  188.9 10.6 %all_to_all.41 = f32[8,32,256]{2,1,0:T(8,128)} all-to-all(f32[8,32,256]{2,1,0:T(8,128)S(1)} %tile.4), channel_id=1, replica_groups=mesh['row'=32,'col'=8] {'col'}, dimensions={0} | all-to-all | bytes 524288 | tf_op jit(solution)/shard_map/all_to_all | solution.py:216
  199.5 12.2 %orthonormal.2 = (bf16[384,256]{1,0:T(8,128)(2,1)}, f32[1,256]{1,0:T(1,128)}) custom-call(f32[256,256]{1,0:T(8,128)} %bitcast.14, f32[384,256]{1,0:T(8,128)} %get-tuple-element.10.z_ref), custom_call_target="tpu_custom_call" | custom-call | tf_op jit(solution)/shard_map/orthonormal/pallas_call | solution.py:192
  211.7 2.1 collective-permute-start.7
  213.8 4.4 %collective-permute-done.7 = bf16[384,256]{1,0:T(8,128)(2,1)S(1)} collective-permute-done((bf16[384,256]{1,0:T(8,128)(2,1)}, bf16[384,256]{1,0:T(8,128)(2,1)S(1)}, u32[]{:S(2)}, u32[]{:S(2)}) %collective-permute-start.7) | collective-permute-done | bytes 196640 | tf_op jit(solution)/shard_map/ppermute | solution.py:246
  218.2 1.7 pad_maximum_fusion.1
  219.9 32.1 %all-gather.5.cloned.1.call-done.x_ref = bf16[6144,256]{1,0:T(8,128)(2,1)} async-done(((bf16[768,256]{1,0:T(8,128)(2,1)}), bf16[6144,256]{1,0:T(8,128)(2,1)}) %all-gather.5.cloned.1.call-update) | async-done | bytes 3145744 | tf_op jit(solution)/shard_map/all_gather | solution.py:247
  252.1 1.9 copy-done.3
  254.0 17.6 %band.3 = bf16[6144,256]{1,0:T(8,128)(2,1)S(1)} custom-call(s32[48]{0:T(128)S(1)} %reshape.61.nb_ref, bf16[8,3,2,128,256]{4,3,2,1,0:T(8,128)(2,1)S(1)} %bitcast.11, bf16[6144,256]{1,0:T(8,128)(2,1)S(1)} %copy-done.3), custom_call_target="tpu_custom_call" | custom-call | tf_op jit(solution)/shard_map/band/pallas_call | solution.py:78
  271.6 1.6 copy-done.1
  273.2 38.5 %reduce-scatter.5.cloned.1.call-done.rs_ref = bf16[768,256]{1,0:T(8,128)(2,1)} async-done(((bf16[6144,256]{1,0:T(8,128)(2,1)}), bf16[768,256]{1,0:T(8,128)(2,1)}) %reduce-scatter.5.cloned.1.call-update) | async-done | bytes 393232 | tf_op jit(solution)/shard_map/reduce_scatter | solution.py:251
  312.7 1.5 collective-permute-start.8
  314.1 4.3 %collective-permute-done.8.got_ref = bf16[384,256]{1,0:T(8,128)(2,1)S(1)} collective-permute-done((bf16[384,256]{1,0:T(8,128)(2,1)S(1)}, bf16[384,256]{1,0:T(8,128)(2,1)S(1)}, u32[]{:S(2)}, u32[]{:S(2)}) %collective-permute-start.8) | collective-permute-done | bytes 196640 | tf_op jit(solution)/shard_map/ppermute | solution.py:252
  319.1 2.4 gram.3
  321.5 10.8 %all_to_all.42 = f32[8,32,256]{2,1,0:T(8,128)S(1)} all-to-all(f32[8,32,256]{2,1,0:T(8,128)} %bitcast.17), channel_id=1, replica_groups=mesh['row'=32,'col'=8] {'col'}, dimensions={0} | all-to-all | bytes 524288 | tf_op jit(solution)/shard_map/all_to_all | solution.py:210
  332.3 4.0 %collective-permute-start.9 = (f32[32,256]{1,0:T(8,128)S(1)}, f32[32,256]{1,0:T(8,128)S(1)}, u32[]{:S(2)}, u32[]{:S(2)}) collective-permute-start(f32[32,256]{1,0:T(8,128)S(1)} %reduce_sum.19), channel_id=1, source_target_pairs={{0,8},{8,0},{16,24},{24,16},{32,40},{40,32},{48,56},{56,48},{64,72... | collective-permute-start | bytes 98312 | tf_op jit(solution)/shard_map/ppermute | solution.py:204
  336.3 1.9 collective-permute-done.9
  338.2 1.0 collective-permute-start.10
  339.3 4.4 %collective-permute-done.10 = f32[32,256]{1,0:T(8,128)S(1)} collective-permute-done((f32[32,256]{1,0:T(8,128)S(1)}, f32[32,256]{1,0:T(8,128)S(1)}, u32[]{:S(2)}, u32[]{:S(2)}) %collective-permute-start.10) | collective-permute-done | bytes 32800 | tf_op jit(solution)/shard_map/ppermute | solution.py:204
  343.9 4.0 %collective-permute-done.11 = f32[32,256]{1,0:T(8,128)S(1)} collective-permute-done((f32[32,256]{1,0:T(8,128)S(1)}, f32[32,256]{1,0:T(8,128)S(1)}, u32[]{:S(2)}, u32[]{:S(2)}) %collective-permute-start.11) | collective-permute-done | bytes 32800 | tf_op jit(solution)/shard_map/ppermute | solution.py:204
  347.9 0.9 collective-permute-start.12
  348.9 3.9 collective-permute-done.12
  352.8 5.6 %collective-permute-start.13 = (f32[32,256]{1,0:T(8,128)S(1)}, f32[32,256]{1,0:T(8,128)S(1)}, u32[]{:S(2)}, u32[]{:S(2)}) collective-permute-start(f32[32,256]{1,0:T(8,128)S(1)} %add.44), channel_id=1, source_target_pairs={{0,128},{8,136},{16,144},{24,152},{32,160},{40,168},{48,176},{56,1... | collective-permute-start | bytes 98312 | tf_op jit(solution)/shard_map/ppermute | solution.py:204
  358.4 2.2 collective-permute-done.13
  360.6 10.6 %all_to_all.43 = f32[8,32,256]{2,1,0:T(8,128)} all-to-all(f32[8,32,256]{2,1,0:T(8,128)S(1)} %tile.5), channel_id=1, replica_groups=mesh['row'=32,'col'=8] {'col'}, dimensions={0} | all-to-all | bytes 524288 | tf_op jit(solution)/shard_map/all_to_all | solution.py:216
  371.2 12.2 %orthonormal.3 = (f32[384,256]{1,0:T(8,128)}, f32[1,256]{1,0:T(1,128)}) custom-call(f32[256,256]{1,0:T(8,128)} %bitcast.15, f32[384,256]{1,0:T(8,128)} %get-tuple-element.13.z_ref), custom_call_target="tpu_custom_call" | custom-call | tf_op jit(solution)/shard_map/orthonormal/pallas_call | solution.py:192
  (46 shorter events, 5.5 us)
Async XLA Ops:
  7.2 71.5 %all-gather.3.cloned.1.call-start = ((), (), s32[]{:S(2)}) async-start(), calls=%async_computation.7 | async-start | bytes 3538944 | tf_op jit(solution)/shard_map/all_gather | solution.py:247
  7.2 6.9 %collective-permute-start = (bf16[384,256]{1,0:T(8,128)(2,1)}, bf16[384,256]{1,0:T(8,128)(2,1)S(1)}, u32[]{:S(2)}, u32[]{:S(2)}) collective-permute-start(bf16[384,256]{1,0:T(8,128)(2,1)} %param.5), channel_id=1, source_target_pairs={{0,248},{1,249},{2,250},{3,251},{4,12},{5,13},{6,14},{7,15},{8,0},... | collective-permute-start | bytes 589832 | tf_op jit(solution)/shard_map/ppermute | solution.py:246
  15.9 2.2 copy-start.7
  15.9 124.1 %reduce-scatter.3.cloned.1.call-start = ((), (), s32[]{:S(2)}) async-start(), calls=%async_computation.8 | async-start | bytes 3538944 | tf_op jit(solution)/shard_map/reduce_scatter | solution.py:251
  74.8 1.7 copy-start.4
  78.7 1.9 copy-start.2
  98.1 1.6 copy-start
  99.8 152.3 %all-gather.5.cloned.1.call-start = ((), (), s32[]{:S(2)}) async-start(), calls=%async_computation.9 | async-start | bytes 3538944 | tf_op jit(solution)/shard_map/all_gather | solution.py:247
  140.9 5.7 %collective-permute-start.1 = (bf16[384,256]{1,0:T(8,128)(2,1)S(1)}, bf16[384,256]{1,0:T(8,128)(2,1)S(1)}, u32[]{:S(2)}, u32[]{:S(2)}) collective-permute-start(bf16[384,256]{1,0:T(8,128)(2,1)S(1)} %slice.18), channel_id=1, source_target_pairs={{248,0},{249,1},{250,2},{251,3},{12,4},{13,5},{14,6},{15,7},{0,8},... | collective-permute-start | bytes 589832 | tf_op jit(solution)/shard_map/ppermute | solution.py:252
  146.7 0.7 copy-start.5
  160.6 6.0 %collective-permute-start.2 = (f32[32,256]{1,0:T(8,128)S(1)}, f32[32,256]{1,0:T(8,128)S(1)}, u32[]{:S(2)}, u32[]{:S(2)}) collective-permute-start(f32[32,256]{1,0:T(8,128)S(1)} %reduce_sum.18), channel_id=1, source_target_pairs={{0,8},{8,0},{16,24},{24,16},{32,40},{40,32},{48,56},{56,48},{64,72... | collective-permute-start | bytes 98312 | tf_op jit(solution)/shard_map/ppermute | solution.py:204
  166.6 5.4 %collective-permute-start.3 = (f32[32,256]{1,0:T(8,128)S(1)}, f32[32,256]{1,0:T(8,128)S(1)}, u32[]{:S(2)}, u32[]{:S(2)}) collective-permute-start(f32[32,256]{1,0:T(8,128)S(1)} %add.36), channel_id=1, source_target_pairs={{0,16},{8,24},{16,0},{24,8},{32,48},{40,56},{48,32},{56,40},{64,80... | collective-permute-start | bytes 98312 | tf_op jit(solution)/shard_map/ppermute | solution.py:204
  172.0 4.3 %collective-permute-start.4 = (f32[32,256]{1,0:T(8,128)S(1)}, f32[32,256]{1,0:T(8,128)S(1)}, u32[]{:S(2)}, u32[]{:S(2)}) collective-permute-start(f32[32,256]{1,0:T(8,128)S(1)} %add.37), channel_id=1, source_target_pairs={{0,32},{8,40},{16,48},{24,56},{32,0},{40,8},{48,16},{56,24},{64,96... | collective-permute-start | bytes 98312 | tf_op jit(solution)/shard_map/ppermute | solution.py:204
  176.3 4.8 %collective-permute-start.5 = (f32[32,256]{1,0:T(8,128)S(1)}, f32[32,256]{1,0:T(8,128)S(1)}, u32[]{:S(2)}, u32[]{:S(2)}) collective-permute-start(f32[32,256]{1,0:T(8,128)S(1)} %add.38), channel_id=1, source_target_pairs={{0,64},{8,72},{16,80},{24,88},{32,96},{40,104},{48,112},{56,120},{... | collective-permute-start | bytes 98312 | tf_op jit(solution)/shard_map/ppermute | solution.py:204
  181.1 7.8 %collective-permute-start.6 = (f32[32,256]{1,0:T(8,128)S(1)}, f32[32,256]{1,0:T(8,128)S(1)}, u32[]{:S(2)}, u32[]{:S(2)}) collective-permute-start(f32[32,256]{1,0:T(8,128)S(1)} %add.39), channel_id=1, source_target_pairs={{0,128},{8,136},{16,144},{24,152},{32,160},{40,168},{48,176},{56,1... | collective-permute-start | bytes 98312 | tf_op jit(solution)/shard_map/ppermute | solution.py:204
  211.7 6.5 %collective-permute-start.7 = (bf16[384,256]{1,0:T(8,128)(2,1)}, bf16[384,256]{1,0:T(8,128)(2,1)S(1)}, u32[]{:S(2)}, u32[]{:S(2)}) collective-permute-start(bf16[384,256]{1,0:T(8,128)(2,1)} %get-tuple-element.11), channel_id=1, source_target_pairs={{0,248},{1,249},{2,250},{3,251},{4,12},{5,13},{6,14},{7,15},{8,0},... | collective-permute-start | bytes 589832 | tf_op jit(solution)/shard_map/ppermute | solution.py:246
  219.9 91.8 %reduce-scatter.5.cloned.1.call-start = ((), (), s32[]{:S(2)}) async-start(), calls=%async_computation.10 | async-start | bytes 3538944 | tf_op jit(solution)/shard_map/reduce_scatter | solution.py:251
  252.1 1.9 copy-start.3
  271.5 1.6 copy-start.1
  312.7 5.7 %collective-permute-start.8 = (bf16[384,256]{1,0:T(8,128)(2,1)S(1)}, bf16[384,256]{1,0:T(8,128)(2,1)S(1)}, u32[]{:S(2)}, u32[]{:S(2)}) collective-permute-start(bf16[384,256]{1,0:T(8,128)(2,1)S(1)} %slice.19), channel_id=1, source_target_pairs={{248,0},{249,1},{250,2},{251,3},{12,4},{13,5},{14,6},{15,7},{0,8},... | collective-permute-start | bytes 589832 | tf_op jit(solution)/shard_map/ppermute | solution.py:252
  318.4 0.7 copy-start.6
  332.3 5.9 %collective-permute-start.9 = (f32[32,256]{1,0:T(8,128)S(1)}, f32[32,256]{1,0:T(8,128)S(1)}, u32[]{:S(2)}, u32[]{:S(2)}) collective-permute-start(f32[32,256]{1,0:T(8,128)S(1)} %reduce_sum.19), channel_id=1, source_target_pairs={{0,8},{8,0},{16,24},{24,16},{32,40},{40,32},{48,56},{56,48},{64,72... | collective-permute-start | bytes 98312 | tf_op jit(solution)/shard_map/ppermute | solution.py:204
  338.2 5.4 %collective-permute-start.10 = (f32[32,256]{1,0:T(8,128)S(1)}, f32[32,256]{1,0:T(8,128)S(1)}, u32[]{:S(2)}, u32[]{:S(2)}) collective-permute-start(f32[32,256]{1,0:T(8,128)S(1)} %add.41), channel_id=1, source_target_pairs={{0,16},{8,24},{16,0},{24,8},{32,48},{40,56},{48,32},{56,40},{64,80... | collective-permute-start | bytes 98312 | tf_op jit(solution)/shard_map/ppermute | solution.py:204
  343.7 4.3 %collective-permute-start.11 = (f32[32,256]{1,0:T(8,128)S(1)}, f32[32,256]{1,0:T(8,128)S(1)}, u32[]{:S(2)}, u32[]{:S(2)}) collective-permute-start(f32[32,256]{1,0:T(8,128)S(1)} %add.42), channel_id=1, source_target_pairs={{0,32},{8,40},{16,48},{24,56},{32,0},{40,8},{48,16},{56,24},{64,96... | collective-permute-start | bytes 98312 | tf_op jit(solution)/shard_map/ppermute | solution.py:204
  347.9 4.8 %collective-permute-start.12 = (f32[32,256]{1,0:T(8,128)S(1)}, f32[32,256]{1,0:T(8,128)S(1)}, u32[]{:S(2)}, u32[]{:S(2)}) collective-permute-start(f32[32,256]{1,0:T(8,128)S(1)} %add.43), channel_id=1, source_target_pairs={{0,64},{8,72},{16,80},{24,88},{32,96},{40,104},{48,112},{56,120},{... | collective-permute-start | bytes 98312 | tf_op jit(solution)/shard_map/ppermute | solution.py:204
  352.8 7.8 %collective-permute-start.13 = (f32[32,256]{1,0:T(8,128)S(1)}, f32[32,256]{1,0:T(8,128)S(1)}, u32[]{:S(2)}, u32[]{:S(2)}) collective-permute-start(f32[32,256]{1,0:T(8,128)S(1)} %add.44), channel_id=1, source_target_pairs={{0,128},{8,136},{16,144},{24,152},{32,160},{40,168},{48,176},{56,1... | collective-permute-start | bytes 98312 | tf_op jit(solution)/shard_map/ppermute | solution.py:204
Sparse Core Ops, SparseCore 0:
  16.0 58.3 all-gather.2
  99.9 40.0 reduce-scatter.2
  220.0 32.0 all-gather.4
  273.3 38.3 reduce-scatter.4
